TPU v7x, 32 devices: a whole 2x2x4 slice. The times are simulated.
32 devices in a mesh: band: 2 (over x), grid: 16 (over z, y, core).
Axes of the slice: x: 2, y: 2, z: 4, core: 2. Of those that a mesh axis runs over, the one named last changes fastest.
Arguments:
- orbitals: float32 [64, 64, 12, 128], P('band', 'grid'), may hold values from -700 to 700
- potential: float32 [64, 12, 128], P('grid'), may hold values from 0.2 to 2
Outputs:
- basis: float32 [64, 64, 12, 128], P('band', 'grid')
All inputs are finite; a program needn't handle non-finite values.
Results may differ from a plain program's by a relative error of at most 0.0001.
Values sent between devices are 32-bit elements; how exact they have to be, the bound alone decides.
A program may use at most 64 MiB of HBM per device.

v0:
```python
import jax
import jax.numpy as jnp
from jax import lax
from jax.sharding import PartitionSpec as P

STENCIL = (-205.0 / 72.0, 8.0 / 5.0, -1.0 / 5.0, 8.0 / 315.0, -1.0 / 560.0)
MIDDLE = 6.875
SPREAD = 3.875


def padded_2(cells, sides, width):
    for axis, dim in sides:
        count = lax.axis_size(axis)
        head = lax.slice_in_dim(cells, 0, width, axis=dim)
        tail = lax.slice_in_dim(cells, cells.shape[dim] - width, cells.shape[dim], axis=dim)
        cells = jnp.concatenate(
            [
                lax.ppermute(tail, axis, [(i, (i + 1) % count) for i in range(count)]),
                cells,
                lax.ppermute(head, axis, [((i + 1) % count, i) for i in range(count)]),
            ],
            axis=dim,
        )
    return cells


def from_root(value, axis, source):
    kept = jnp.where(lax.axis_index(axis) == source, value, 0).astype(value.dtype)
    return lax.psum(kept, axis)


def apply_ham(field, potential):
    padded = padded_2(field, (("grid", 1),), 4)
    planes = field.shape[1]
    laplace = 3.0 * STENCIL[0] * field
    for m in range(1, 5):
        beside_all = padded[:, 4 + m : 4 + m + planes] + padded[:, 4 - m : 4 - m + planes]
        beside_all = beside_all + jnp.roll(field, m, 2) + jnp.roll(field, -m, 2)
        beside_all = beside_all + jnp.roll(field, m, 3) + jnp.roll(field, -m, 3)
        laplace = laplace + STENCIL[m] * beside_all
    return -0.5 * laplace + potential[None] * field


def products(left, right):
    return jnp.dot(left, right.T, precision=lax.Precision.HIGHEST)


def on_device(orbitals, potential):
    first_step = (apply_ham(orbitals, potential) - MIDDLE * orbitals) / SPREAD
    second = 2.0 * (apply_ham(first_step, potential) - MIDDLE * first_step) / SPREAD - orbitals
    group_rows = orbitals.shape[0]
    filtered = second.reshape(group_rows, -1)
    total_cells = filtered.shape[1] * lax.axis_size("grid")
    position = lax.axis_index("band")
    groups = lax.axis_size("band")
    result = jnp.zeros_like(filtered)
    residual_block = filtered
    margin = lax.psum(products(filtered, filtered), "grid") / total_cells
    for h in range(groups):
        factor = jnp.linalg.cholesky(margin)
        orthonormal = lax.linalg.triangular_solve(
            factor, residual_block, left_side=True, lower=True
        )
        result = jnp.where(position == h, orthonormal, result)
        if h + 1 < groups:
            finished = from_root(orthonormal, "band", h)
            coeffs = lax.psum(products(finished, residual_block), "grid") / total_cells
            pending = position > h
            residual_block = jnp.where(
                pending,
                residual_block - jnp.dot(coeffs.T, finished, precision=lax.Precision.HIGHEST),
                residual_block,
            )
            margin = jnp.where(
                pending, margin - jnp.dot(coeffs.T, coeffs, precision=lax.Precision.HIGHEST), margin
            )
    return result.reshape(orbitals.shape)


def solution(mesh):
    in_specs = (P("band", "grid", None, None), P("grid", None, None))
    out_specs = P("band", "grid", None, None)
    return jax.shard_map(
        on_device, mesh=mesh, in_specs=in_specs, out_specs=out_specs, check_vma=False
    )
```

profile of v0, /device:TPU:2, one launch (start us, length us, event | category | flops | bytes accessed | tf_op | source)
XLA Modules:
  0.0 254.3 jit_solution(17838417566731010784)
XLA Ops:
  6.5 4.0 %collective-permute-start = (f32[32,4,12,128]{3,1,2,0:T(4,128)}, f32[32,4,12,128]{3,1,2,0:T(4,128)}, u32[]{:S(2)}, u32[]{:S(2)}) collective-permute-start(f32[32,4,12,128]{3,1,2,0:T(4,128)} %param.5), channel_id=1, source_target_pairs={{1,0},{2,1},{3,2},{4,3},{5,4},{6,5},{7,6},{8,7},{9,8},{10,9},{11,1... | collective-permute-start | bytes 2359304 | tf_op jit(solution)/shard_map/ppermute | solution.py:20
  10.5 2.0 fusion.95
  12.5 1.4 fusion.96
  13.9 1.6 fusion.99
  15.5 1.6 fusion.100
  17.1 1.6 fusion.103
  18.7 1.6 fusion.104
  20.3 1.4 fusion.94
  21.7 1.2 fusion.98
  31.8 10.4 %broadcast_multiply_fusion = (f32[32,4,12,128]{3,1,2,0:T(4,128)S(1)}, f32[32,4,12,128]{3,1,2,0:T(4,128)S(1)}) fusion(f32[32,4,12,128]{3,1,2,0:T(4,128)S(1)} %copy-done, f32[4,12,128]{2,0,1:T(4,128)S(1)} %copy-done.11, f32[32,4,12,4]{3,1,2,0:T(4,128)S(1)} %get-tuple-element.70, f32[32,4,12,124]{3,1,2,0:T(4,128)S(1)} %get-tuple-element.72, ...), kind=kLoop, calls=%fused_computation.92 | loop fusion | flops 11206656 | bytes 16539648 | tf_op jit(solution)/shard_map/div | solution.py:49
  45.8 4.5 %collective-permute-start.2 = (f32[32,4,12,128]{3,1,2,0:T(4,128)S(1)}, f32[32,4,12,128]{3,1,2,0:T(4,128)S(1)}, u32[]{:S(2)}, u32[]{:S(2)}) collective-permute-start(f32[32,4,12,128]{3,1,2,0:T(4,128)S(1)} %get-tuple-element.6), channel_id=1, source_target_pairs={{1,0},{2,1},{3,2},{4,3},{5,4},{6,5},{7,6},{8,7},{9,8},{10,9},{11,1... | collective-permute-start | bytes 2359304 | tf_op jit(solution)/shard_map/ppermute | solution.py:20
  51.3 8.5 %collective-permute-done.2 = f32[32,4,12,128]{3,1,2,0:T(4,128)S(1)} collective-permute-done((f32[32,4,12,128]{3,1,2,0:T(4,128)S(1)}, f32[32,4,12,128]{3,1,2,0:T(4,128)S(1)}, u32[]{:S(2)}, u32[]{:S(2)}) %collective-permute-start.2) | collective-permute-done | bytes 786464 | tf_op jit(solution)/shard_map/ppermute | solution.py:20
  59.8 4.6 %collective-permute-done.3 = f32[32,4,12,128]{3,1,2,0:T(4,128)S(1)} collective-permute-done((f32[32,4,12,128]{3,1,2,0:T(4,128)S(1)}, f32[32,4,12,128]{3,1,2,0:T(4,128)S(1)}, u32[]{:S(2)}, u32[]{:S(2)}) %collective-permute-start.3) | collective-permute-done | bytes 786464 | tf_op jit(solution)/shard_map/ppermute | solution.py:18
  64.4 11.5 %multiply_subtract_fusion = f32[32,4,12,128]{3,1,2,0:T(4,128)S(1)} fusion(f32[32,4,12,128]{3,1,2,0:T(4,128)S(1)} %copy-done, f32[32,4,12,128]{3,1,2,0:T(4,128)S(1)} %get-tuple-element.8, f32[32,4,12,4]{3,1,2,0:T(4,128)S(1)} %get-tuple-element.38, f32[32,4,12,124]{3,1,2,0:T(4,128)S(1)} %get-tuple-element.40, f32[32,4,12,124]{3,1,2,0:T(4,128)S(1)} %get-tuple-element.39, ...), kind=kLoop, calls=%fused_computation.90 | loop fusion | flops 11403264 | bytes 17326080 | tf_op jit(solution)/shard_map/sub | solution.py:50
  76.9 57.6 %psum.21 = f32[32,32]{0,1:T(8,128)S(1)} all-reduce(f32[32,32]{0,1:T(8,128)S(1)} %convolution_bitcast_fusion), channel_id=1, replica_groups=mesh['band'=2,'grid'=16] {'grid'}, use_global_device_ids=true, to_apply=%region_0.1 | all-reduce | flops 1024 | bytes 8192 | tf_op jit(solution)/shard_map/psum | solution.py:58
  134.6 2.9 %cholesky.44 = f32[32,32]{1,0:T(8,128)S(1)} custom-call(f32[32,32]{1,0:T(8,128)S(1)} %fusion.68), custom_call_target="Cholesky" | custom-call | tf_op jit(solution)/shard_map/jit(cholesky)/cholesky | solution.py:60
  138.9 2.4 custom-call.6
  141.5 1.7 convolution_select_fusion.1
  143.2 30.5 %all-reduce.2.cloned.1.call-done = f32[32,6144]{1,0:T(8,128)} async-done(((f32[32,6144]{1,0:T(8,128)}), f32[32,6144]{1,0:T(8,128)}) %all-reduce.2.cloned.1.call-update) | async-done | bytes 786448 | tf_op jit(solution)/shard_map/psum | solution.py:29
  173.7 2.0 fusion.109
  175.7 61.4 %psum.23 = f32[32,32]{0,1:T(8,128)S(1)} all-reduce(f32[32,32]{0,1:T(8,128)S(1)} %fusion.109), channel_id=1, replica_groups=mesh['band'=2,'grid'=16] {'grid'}, use_global_device_ids=true, to_apply=%region_4.7 | all-reduce | flops 1024 | bytes 8192 | tf_op jit(solution)/shard_map/psum | solution.py:67
  237.4 2.9 %cholesky.55 = f32[32,32]{1,0:T(8,128)S(1)} custom-call(f32[32,32]{1,0:T(8,128)S(1)} %fusion.66), custom_call_target="Cholesky" | custom-call | tf_op jit(solution)/shard_map/jit(cholesky)/cholesky | solution.py:60
  241.7 2.4 custom-call.7
  246.3 1.2 copy.19
  (73 shorter events, 19.6 us)
Async XLA Ops:
  6.5 6.0 %copy-start = (f32[32,4,12,128]{3,1,2,0:T(4,128)S(1)}, f32[32,4,12,128]{3,1,2,0:T(4,128)}, u32[]{:S(2)}) copy-start(f32[32,4,12,128]{3,1,2,0:T(4,128)} %param.5) | copy-start | bytes 2359300
  6.5 167.2 %all-reduce.2.cloned.1.call-start = ((), (), s32[]{:S(2)}) async-start(), calls=%async_computation | async-start | bytes 1572864 | tf_op jit(solution)/shard_map/psum | solution.py:29
  6.5 23.3 %collective-permute-start = (f32[32,4,12,128]{3,1,2,0:T(4,128)}, f32[32,4,12,128]{3,1,2,0:T(4,128)}, u32[]{:S(2)}, u32[]{:S(2)}) collective-permute-start(f32[32,4,12,128]{3,1,2,0:T(4,128)} %param.5), channel_id=1, source_target_pairs={{1,0},{2,1},{3,2},{4,3},{5,4},{6,5},{7,6},{8,7},{9,8},{10,9},{11,1... | collective-permute-start | bytes 2359304 | tf_op jit(solution)/shard_map/ppermute | solution.py:20
  10.5 19.3 %collective-permute-start.1 = (f32[32,4,12,128]{3,1,2,0:T(4,128)}, f32[32,4,12,128]{3,1,2,0:T(4,128)}, u32[]{:S(2)}, u32[]{:S(2)}) collective-permute-start(f32[32,4,12,128]{3,1,2,0:T(4,128)} %param.5), channel_id=1, source_target_pairs={{0,1},{1,2},{2,3},{3,4},{4,5},{5,6},{6,7},{7,8},{8,9},{9,10},{10,1... | collective-permute-start | bytes 2359304 | tf_op jit(solution)/shard_map/ppermute | solution.py:18
  28.8 1.1 copy-start.6
  28.8 1.4 copy-start.7
  28.8 1.6 copy-start.8
  28.9 1.8 copy-start.9
  29.3 1.7 copy-start.2
  29.3 1.9 copy-start.3
  29.4 2.2 copy-start.4
  29.4 2.4 copy-start.5
  29.4 2.4 copy-start.11
  45.8 14.0 %collective-permute-start.2 = (f32[32,4,12,128]{3,1,2,0:T(4,128)S(1)}, f32[32,4,12,128]{3,1,2,0:T(4,128)S(1)}, u32[]{:S(2)}, u32[]{:S(2)}) collective-permute-start(f32[32,4,12,128]{3,1,2,0:T(4,128)S(1)} %get-tuple-element.6), channel_id=1, source_target_pairs={{1,0},{2,1},{3,2},{4,3},{5,4},{6,5},{7,6},{8,7},{9,8},{10,9},{11,1... | collective-permute-start | bytes 2359304 | tf_op jit(solution)/shard_map/ppermute | solution.py:20
  50.3 14.1 %collective-permute-start.3 = (f32[32,4,12,128]{3,1,2,0:T(4,128)S(1)}, f32[32,4,12,128]{3,1,2,0:T(4,128)S(1)}, u32[]{:S(2)}, u32[]{:S(2)}) collective-permute-start(f32[32,4,12,128]{3,1,2,0:T(4,128)S(1)} %get-tuple-element.6), channel_id=1, source_target_pairs={{0,1},{1,2},{2,3},{3,4},{4,5},{5,6},{6,7},{7,8},{8,9},{9,10},{10,1... | collective-permute-start | bytes 2359304 | tf_op jit(solution)/shard_map/ppermute | solution.py:18
  173.7 70.4 %copy-start.10 = (f32[32,6144]{1,0:T(8,128)S(1)}, f32[32,6144]{1,0:T(8,128)}, u32[]{:S(2)}) copy-start(f32[32,6144]{1,0:T(8,128)} %all-reduce.2.cloned.1.call-done) | copy-start | bytes 2359300
  244.1 1.2 copy-start.1
Sparse Core Ops, SparseCore 0:
  143.3 30.3 all-reduce.1
where the time goes:
time: 257 us; the launch traced here: 254 us
  blocking collectives  119 us (46%)
  waiting for transfers between devices  43.7 us (17%)
  other arithmetic  36 us (14%)
  local copies, waits for them, and re-layouts  27 us (11%)
  between operations  13.7 us (5%)
  starting transfers between devices  8.5 us (3%)
  matrix products  6.39 us (2%)
    psum x1, blocking collectives, on_device(): coeffs = lax.psum(products(finished, residual_block), 'grid') / total_cells  61.4 us
    psum x1, blocking collectives, on_device(): margin = lax.psum(products(filtered, filtered), 'grid') / total_cells  57.6 us
    psum x1, waiting for transfers between devices, from_root(): return lax.psum(kept, axis)  30.5 us
    slice x16, local copies, waits for them, and re-layouts, apply_ham(): beside_all = beside_all + jnp.roll(field, m, 3) + jnp.roll(field, -m, 3)  14.5 us
    sub x1, other arithmetic, on_device(): 2.0 * (apply_ham(first_step, potential) - MIDDLE * first_step) / SPREAD  11.5 us
    div x1, other arithmetic, on_device(): first_step = (apply_ham(orbitals, potential) - MIDDLE * orbitals) / SPREAD  10.4 us
    ppermute x2, waiting for transfers between devices, padded_2(): lax.ppermute(head, axis, [((i + 1) % count, i) for i in range(count)])  8.53 us
    slice x16, local copies, waits for them, and re-layouts, apply_ham(): beside_all = beside_all + jnp.roll(field, m, 2) + jnp.roll(field, -m, 2)  8.52 us
  transfers between devices with their start and end apart: 5, of which 3 were waited for; matrix products, arithmetic and copies ran while one was open for 8% of the time, Pallas kernels for 0%

commit v1 on v0

--- a/solution.py
+++ b/solution.py
@@ -1,11 +1,17 @@
+import functools
+
 import jax
 import jax.numpy as jnp
 from jax import lax
+from jax.experimental import pallas as pl
+from jax.experimental.pallas import tpu as pltpu
 from jax.sharding import PartitionSpec as P
 
 STENCIL = (-205.0 / 72.0, 8.0 / 5.0, -1.0 / 5.0, 8.0 / 315.0, -1.0 / 560.0)
 MIDDLE = 6.875
 SPREAD = 3.875
+ROWS = 8
+MESH = pl.DeviceIdType.MESH
 
 
 def padded_2(cells, sides, width):
@@ -45,7 +51,7 @@
     return jnp.dot(left, right.T, precision=lax.Precision.HIGHEST)
 
 
-def on_device(orbitals, potential):
+def on_device_any(orbitals, potential):
     first_step = (apply_ham(orbitals, potential) - MIDDLE * orbitals) / SPREAD
     second = 2.0 * (apply_ham(first_step, potential) - MIDDLE * first_step) / SPREAD - orbitals
     group_rows = orbitals.shape[0]
@@ -77,7 +83,252 @@
     return result.reshape(orbitals.shape)
 
 
+def chebyshev_step(ext, pot_ref, c, p):
+    here = ext[c, 4 + p]
+    ny = here.shape[0]
+    pot = pot_ref[p].reshape(ny, 1, here.shape[2])
+    out = here * ((pot - (MIDDLE + 1.5 * STENCIL[0])) / SPREAD)
+    for m in range(1, 5):
+        beside = ext[c, 4 + p + m] + ext[c, 4 + p - m]
+        beside = beside + jnp.concatenate([here[ny - m :], here[: ny - m]], axis=0)
+        beside = beside + jnp.concatenate([here[m:], here[:m]], axis=0)
+        beside = beside + pltpu.roll(here, m, 2) + pltpu.roll(here, here.shape[2] - m, 2)
+        out = out + (-0.5 * STENCIL[m] / SPREAD) * beside
+    return out
+
+
+def inverse_factor(gram):
+    size = gram.shape[0]
+    lanes = lax.broadcasted_iota(jnp.int32, (ROWS, 2 * size), 1)
+    rows = lax.broadcasted_iota(jnp.int32, (ROWS, 2 * size), 0)
+    unit_rows = lax.broadcasted_iota(jnp.int32, (size, size), 0)
+    unit_lanes = lax.broadcasted_iota(jnp.int32, (size, size), 1)
+    unit = jnp.where(unit_rows == unit_lanes, 1.0, 0.0).astype(jnp.float32)
+    whole = jnp.concatenate([gram, unit], axis=1)
+    blocks = [whole[ROWS * k : ROWS * (k + 1)] for k in range(size // ROWS)]
+    for j in range(size):
+        own, at = divmod(j, ROWS)
+        row = blocks[own][at : at + 1]
+        row = row / row[:, j : j + 1]
+        for k in range(own, size // ROWS):
+            less = blocks[k] - blocks[k][:, j : j + 1] * row
+            blocks[k] = jnp.where(rows > at, less, blocks[k]) if k == own else less
+    scaled = []
+    for k, block in enumerate(blocks):
+        pivot = jnp.sum(jnp.where(lanes == rows + ROWS * k, block, 0.0), axis=1, keepdims=True)
+        scaled.append(block[:, size:] / jnp.sqrt(pivot))
+    return jnp.concatenate(scaled, axis=0)
+
+
+def split(value):
+    high = value.astype(jnp.bfloat16)
+    return high, (value - high.astype(jnp.float32)).astype(jnp.bfloat16)
+
+
+def kernel(
+    n, x_ref, pot_ref, out_ref,
+    ext, ext2, fil, fil0, both, near, far,
+    send1, recv1, send2, recv2, sendx, recvx, sendn, recvn, sendf, recvf,
+):
+    chunks, planes, ny = x_ref.shape[:3]
+    lines = planes * ny
+    me = lax.axis_index("grid")
+    band = lax.axis_index("band")
+    right, left = lax.rem(me + 1, n), lax.rem(me + n - 1, n)
+    inner = 4
+    outer = n // inner
+    q, zz = lax.rem(me, inner), lax.div(me, inner)
+    near_peers = [zz * inner + lax.rem(q + k, inner) for k in range(1, inner)]
+    far_peers = [lax.rem(zz + k, outer) * inner + q for k in range(1, outer)]
+    partner = {"band": 1 - band}
+
+    barrier = pltpu.get_barrier_semaphore()
+    peers = [{"grid": d} for d in [left, right] + near_peers + far_peers] + [partner]
+    for peer in peers:
+        pl.semaphore_signal(barrier, inc=1, device_id=peer, device_id_type=MESH)
+    pl.semaphore_wait(barrier, len(peers))
+
+    own = pl.ds(4, planes)
+
+    def halo(src, dst, send, recv, c, side):
+        where = pl.ds(0, 4) if side == 0 else pl.ds(4 + planes, 4)
+        return pltpu.make_async_remote_copy(
+            src_ref=src, dst_ref=dst.at[c, where],
+            send_sem=send.at[side, c], recv_sem=recv.at[side, c],
+            device_id={"grid": right if side == 0 else left}, device_id_type=MESH,
+        )
+
+    def halo1(c, side):
+        return halo(x_ref.at[c], ext, send1, recv1, c, side)
+
+    def halo2(c, side):
+        return halo(ext2.at[c, own], ext2, send2, recv2, c, side)
+
+    def across(c):
+        return pltpu.make_async_remote_copy(
+            src_ref=fil.at[c], dst_ref=fil0.at[c],
+            send_sem=sendx.at[c], recv_sem=recvx.at[c],
+            device_id=partner, device_id_type=MESH,
+        )
+
+    def begin(c, carry):
+        halo1(c, 0).start()
+        halo1(c, 1).start()
+        ext[c, own] = x_ref[c]
+        return carry
+
+    lax.fori_loop(0, chunks, begin, 0)
+
+    def first(c, carry):
+        halo1(c, 0).wait_recv()
+        halo1(c, 1).wait_recv()
+        for p in range(planes):
+            ext2[c, 4 + p] = chebyshev_step(ext, pot_ref, c, p)
+        halo2(c, 0).start()
+        halo2(c, 1).start()
+        return carry
+
+    lax.fori_loop(0, chunks, first, 0)
+
+    def second(c, carry):
+        halo2(c, 0).wait_recv()
+        halo2(c, 1).wait_recv()
+        for p in range(planes):
+            value = 2.0 * chebyshev_step(ext2, pot_ref, c, p) - ext[c, 4 + p]
+            fil[c, pl.ds(p * ny, ny)] = value
+
+        @pl.when(band == 0)
+        def _():
+            across(c).start()
+            fil0[c] = fil[c]
+
+        return carry
+
+    lax.fori_loop(0, chunks, second, 0)
+
+    @pl.when(band == 1)
+    def _():
+        for c in range(chunks):
+            across(c).wait_recv()
+
+    rows = chunks * ROWS
+    size = 2 * rows
+
+    def pair(i):
+        def at(ref, line):
+            return ref[:, line].reshape(rows, ref.shape[3])
+
+        return jnp.concatenate(
+            [
+                jnp.concatenate([at(fil0, 2 * i + t), at(fil, 2 * i + t)], axis=0)
+                for t in range(2)
+            ],
+            axis=1,
+        )
+
+    def gram(i, total):
+        high, low = split(pair(i))
+        tall = jnp.concatenate([high, low], axis=0)
+        both[i] = tall
+        return total + lax.dot_general(
+            tall, tall, (((1,), (1,)), ((), ())), preferred_element_type=jnp.float32
+        )
+
+    total = lax.fori_loop(0, lines // 2, gram, jnp.zeros((2 * size, 2 * size), jnp.float32))
+    total = total[:size] + total[size:]
+    total = total[:, :size] + total[:, size:]
+    packed = jnp.concatenate([total[:rows], total[rows:]], axis=1)
+
+    def exchange(value, slots, send, recv, place, peers, sources):
+        slots[place] = value
+        copies = [
+            pltpu.make_async_remote_copy(
+                src_ref=slots.at[place], dst_ref=slots.at[place],
+                send_sem=send.at[k], recv_sem=recv.at[k],
+                device_id={"grid": peer}, device_id_type=MESH,
+            )
+            for k, peer in enumerate(peers)
+        ]
+        for copy in copies:
+            copy.start()
+        for copy in copies:
+            copy.wait_send()
+        for k, source in enumerate(sources):
+            pltpu.make_async_remote_copy(
+                src_ref=slots.at[source], dst_ref=slots.at[source],
+                send_sem=send.at[k], recv_sem=recv.at[k],
+                device_id={"grid": peers[k]}, device_id_type=MESH,
+            ).wait_recv()
+        out = slots[0]
+        for k in range(1, slots.shape[0]):
+            out = out + slots[k]
+        return out
+
+    near_from = [lax.rem(q + inner - k, inner) for k in range(1, inner)]
+    far_from = [lax.rem(zz + outer - k, outer) for k in range(1, outer)]
+    packed = exchange(packed, near, sendn, recvn, q, near_peers, near_from)
+    packed = exchange(packed, far, sendf, recvf, zz, far_peers, far_from)
+    packed = packed / (lines * x_ref.shape[4] * n)
+    inverse = inverse_factor(jnp.concatenate([packed[:, :size], packed[:, size:]], axis=0))
+    weights = jnp.where(band == 0, inverse[:rows], inverse[rows:])
+    high, low = split(weights)
+    tall = jnp.concatenate([high, low], axis=0)
+    wide = jnp.concatenate([tall, tall], axis=1)
+
+    def final(i, carry):
+        out = jnp.dot(wide, both[i], preferred_element_type=jnp.float32)
+        out = out[:rows] + out[rows:]
+        half = out.shape[1] // 2
+        out_ref[2 * i] = out[:, :half]
+        out_ref[2 * i + 1] = out[:, half:]
+        return carry
+
+    lax.fori_loop(0, lines // 2, final, 0)
+
+    for c in range(chunks):
+        for side in range(2):
+            halo1(c, side).wait_send()
+            halo2(c, side).wait_send()
+
+    @pl.when(band == 0)
+    def _():
+        for c in range(chunks):
+            across(c).wait_send()
+
+
+def on_device_two(n, orbitals, potential):
+    rows, planes, ny, nz = orbitals.shape
+    chunks = rows // ROWS
+    x = orbitals.reshape(chunks, ROWS, planes, ny, nz).transpose(0, 2, 3, 1, 4)
+    f32, dma = jnp.float32, pltpu.SemaphoreType.DMA
+    out = pl.pallas_call(
+        functools.partial(kernel, n),
+        out_shape=jax.ShapeDtypeStruct((planes * ny, rows, nz), f32),
+        in_specs=[pl.BlockSpec(memory_space=pltpu.VMEM)] * 2,
+        out_specs=pl.BlockSpec(memory_space=pltpu.VMEM),
+        scratch_shapes=[
+            pltpu.VMEM((chunks, planes + 8, ny, ROWS, nz), f32),
+            pltpu.VMEM((chunks, planes + 8, ny, ROWS, nz), f32),
+            pltpu.VMEM((chunks, planes * ny, ROWS, nz), f32),
+            pltpu.VMEM((chunks, planes * ny, ROWS, nz), f32),
+            pltpu.VMEM((planes * ny // 2, 4 * rows, 2 * nz), jnp.bfloat16),
+            pltpu.VMEM((4, rows, 4 * rows), f32),
+            pltpu.VMEM((n // 4, rows, 4 * rows), f32),
+            dma((2, chunks)), dma((2, chunks)), dma((2, chunks)), dma((2, chunks)),
+            dma((chunks,)), dma((chunks,)),
+            dma((3,)), dma((3,)), dma((n // 4 - 1,)), dma((n // 4 - 1,)),
+        ],
+        compiler_params=pltpu.CompilerParams(
+            collective_id=0, has_side_effects=True, vmem_limit_bytes=40 * 1024 * 1024
+        ),
+    )(x, potential)
+    return out.reshape(planes, ny, rows, nz).transpose(2, 0, 1, 3)
+
+
 def solution(mesh):
+    n = mesh.shape["grid"]
+    one_kernel = mesh.shape["band"] == 2 and n % 4 == 0 and n > 4
+    on_device = functools.partial(on_device_two, n) if one_kernel else on_device_any
     in_specs = (P("band", "grid", None, None), P("grid", None, None))
     out_specs = P("band", "grid", None, None)
     return jax.shard_map(

time: 257 us -> 68.5 us (0.27)
  blocking collectives: 119 us -> 0 us
  Pallas kernels: 0 us -> 64.8 us
  waiting for transfers between devices: 43.7 us -> 0 us
  other arithmetic: 36 us -> 0 us
  local copies, waits for them, and re-layouts: 27 us -> 3.5 us
  between operations: 13.7 us -> 0.01 us
  starting transfers between devices: 8.5 us -> 0 us
  matrix products: 6.39 us -> 0 us
    psum x2 -> x0, blocking collectives: 119 us -> none  [the longest x1 61.4 us: on_device(): coeffs = lax.psum(products(finished, residual_block), 'grid') / total_cells]
    pallas_call x0 -> x1, Pallas kernels: none -> 64.8 us  [on_device_two(): pl.pallas_call(functools.partial(kernel, n), out_shape=jax.ShapeDtypeStru...]
    psum x1 -> x0, waiting for transfers between devices: 30.5 us -> none  [from_root(): return lax.psum(kept, axis)]
    slice x32 -> x0, local copies, waits for them, and re-layouts: 23 us -> none  [the longest x16 14.5 us: apply_ham(): beside_all = beside_all + jnp.roll(field, m, 3) + jnp.roll(field, -m, 3)]
    another operation x10 -> x0, other arithmetic: 13.4 us -> none  [the longest x6 7.23 us: on_device(): factor = jnp.linalg.cholesky(margin)]
    ppermute x4 -> x0, waiting for transfers between devices: 13.1 us -> none  [the longest x2 8.53 us: padded_2(): lax.ppermute(head, axis, [((i + 1) % count, i) for i in range(count)])]
    sub x1 -> x0, other arithmetic: 11.5 us -> none  [on_device(): 2.0 * (apply_ham(first_step, potential) - MIDDLE * first_step) / SPREAD]
    div x4 -> x0, other arithmetic: 10.4 us -> none  [the longest x1 10.4 us: on_device(): first_step = (apply_ham(orbitals, potential) - MIDDLE * orbitals) / SPREAD]
  transfers between devices with their start and end apart: 5 -> 0, of which waited for: 3 -> 0; matrix products, arithmetic and copies ran while one was open for 8% -> 0% of each run, Pallas kernels for 0% -> 0%
where the time goes in v1:
time: 68.5 us; the launch traced here: 68.3 us
  Pallas kernels  64.8 us (95%)
  local copies, waits for them, and re-layouts  3.5 us (5%)
    pallas_call x1, Pallas kernels, on_device_two(): pl.pallas_call(functools.partial(kernel, n), out_shape=jax.ShapeDtypeStru...  64.8 us
    reshape x1, local copies, waits for them, and re-layouts, on_device_two(): return out.reshape(planes, ny, rows, nz).transpose(2, 0, 1, 3)  1.39 us
    reshape x1, local copies, waits for them, and re-layouts, on_device_two(): x = orbitals.reshape(chunks, ROWS, planes, ny, nz).transpose(0, 2, 3, 1, 4)  1.38 us

profile of v1, /device:TPU:2, one launch (start us, length us, event | category | flops | bytes accessed | tf_op | source)
XLA Modules:
  0.0 68.3 jit_solution(12466978781685399956)
XLA Ops:
  0.0 0.7 %copy.7.pot_ref = f32[4,12,128]{2,1,0:T(8,128)S(1)} copy(f32[4,12,128]{2,0,1:T(4,128)} %param.3) | data formatting | bytes 49152 | tf_op args[1]
  0.7 1.4 %copy.13 = f32[4,8,4,12,128]{4,1,3,2,0:T(8,128)S(1)} copy(f32[4,8,4,12,128]{4,2,3,1,0:T(4,128)} %bitcast.10) | data formatting | bytes 1572864 | tf_op jit(solution)/shard_map/reshape | solution.py:302
  2.1 64.8 %shard_map.28 = f32[48,32,128]{2,1,0:T(8,128)S(1)} custom-call(f32[4,4,12,8,128]{4,3,2,1,0:T(8,128)S(1)} %bitcast.9, f32[4,12,128]{2,1,0:T(8,128)S(1)} %copy.7.pot_ref), custom_call_target="tpu_custom_call" | custom-call | tf_op jit(solution)/shard_map/pallas_call | solution.py:304
  66.9 1.4 %copy.14 = f32[4,12,32,128]{3,0,1,2:T(4,128)} copy(f32[4,12,32,128]{3,2,1,0:T(8,128)S(1)} %bitcast.8) | data formatting | bytes 1572864 | tf_op jit(solution)/shard_map/reshape | solution.py:325

commit v2 on v1

--- a/solution.py
+++ b/solution.py
@@ -11,6 +11,7 @@
 MIDDLE = 6.875
 SPREAD = 3.875
 ROWS = 8
+UNROLL = 12
 MESH = pl.DeviceIdType.MESH
 
 
@@ -86,7 +87,7 @@
 def chebyshev_step(ext, pot_ref, c, p):
     here = ext[c, 4 + p]
     ny = here.shape[0]
-    pot = pot_ref[p].reshape(ny, 1, here.shape[2])
+    pot = pot_ref[:, p : p + 1, :]
     out = here * ((pot - (MIDDLE + 1.5 * STENCIL[0])) / SPREAD)
     for m in range(1, 5):
         beside = ext[c, 4 + p + m] + ext[c, 4 + p - m]
@@ -106,13 +107,24 @@
     unit = jnp.where(unit_rows == unit_lanes, 1.0, 0.0).astype(jnp.float32)
     whole = jnp.concatenate([gram, unit], axis=1)
     blocks = [whole[ROWS * k : ROWS * (k + 1)] for k in range(size // ROWS)]
-    for j in range(size):
+    for j in range(0, size, 2):
         own, at = divmod(j, ROWS)
-        row = blocks[own][at : at + 1]
-        row = row / row[:, j : j + 1]
+        row0, row1 = blocks[own][at : at + 1], blocks[own][at + 1 : at + 2]
+        scale = 1.0 / row0[:, j : j + 1]
+        across = row0[:, j + 1 : j + 2]
+        ratio = row1[:, j : j + 1] * scale
+        row1_left = row1 - ratio * row0
+        cross = across * scale
+        unit0 = row0 * scale
+        unit1 = row1_left / (row1[:, j + 1 : j + 2] - ratio * across)
         for k in range(own, size // ROWS):
-            less = blocks[k] - blocks[k][:, j : j + 1] * row
-            blocks[k] = jnp.where(rows > at, less, blocks[k]) if k == own else less
+            col0 = blocks[k][:, j : j + 1]
+            col1 = blocks[k][:, j + 1 : j + 2] - col0 * cross
+            less = blocks[k] - col0 * unit0 - col1 * unit1
+            if k == own:
+                less = jnp.where(rows > at + 1, less, blocks[k])
+                less = jnp.where(rows == at + 1, row1_left, less)
+            blocks[k] = less
     scaled = []
     for k, block in enumerate(blocks):
         pivot = jnp.sum(jnp.where(lanes == rows + ROWS * k, block, 0.0), axis=1, keepdims=True)
@@ -234,7 +246,9 @@
             tall, tall, (((1,), (1,)), ((), ())), preferred_element_type=jnp.float32
         )
 
-    total = lax.fori_loop(0, lines // 2, gram, jnp.zeros((2 * size, 2 * size), jnp.float32))
+    total = lax.fori_loop(
+        0, lines // 2, gram, jnp.zeros((2 * size, 2 * size), jnp.float32), unroll=UNROLL
+    )
     total = total[:size] + total[size:]
     total = total[:, :size] + total[:, size:]
     packed = jnp.concatenate([total[:rows], total[rows:]], axis=1)
@@ -283,7 +297,7 @@
         out_ref[2 * i + 1] = out[:, half:]
         return carry
 
-    lax.fori_loop(0, lines // 2, final, 0)
+    lax.fori_loop(0, lines // 2, final, 0, unroll=UNROLL)
 
     for c in range(chunks):
         for side in range(2):
@@ -321,7 +335,7 @@
         compiler_params=pltpu.CompilerParams(
             collective_id=0, has_side_effects=True, vmem_limit_bytes=40 * 1024 * 1024
         ),
-    )(x, potential)
+    )(x, potential.transpose(1, 0, 2))
     return out.reshape(planes, ny, rows, nz).transpose(2, 0, 1, 3)
 
 

time: 68.5 us -> 65.3 us (0.953)
  Pallas kernels: 64.8 us -> 62.3 us
  local copies, waits for them, and re-layouts: 3.5 us -> 2.77 us
    pallas_call x1, Pallas kernels: 64.8 us -> 62.3 us  [on_device_two(): pl.pallas_call(functools.partial(kernel, n), out_shape=jax.ShapeDtypeStru...]
    unnamed x1 -> x2, local copies, waits for them, and re-layouts: 0.74 us -> 0.01 us
where the time goes in v2:
time: 65.3 us; the launch traced here: 65.1 us
  Pallas kernels  62.3 us (95%)
  local copies, waits for them, and re-layouts  2.77 us (4%)
    pallas_call x1, Pallas kernels, on_device_two(): pl.pallas_call(functools.partial(kernel, n), out_shape=jax.ShapeDtypeStru...  62.3 us
    reshape x1, local copies, waits for them, and re-layouts, on_device_two(): return out.reshape(planes, ny, rows, nz).transpose(2, 0, 1, 3)  1.39 us
    reshape x1, local copies, waits for them, and re-layouts, on_device_two(): x = orbitals.reshape(chunks, ROWS, planes, ny, nz).transpose(0, 2, 3, 1, 4)  1.38 us

profile of v2, /device:TPU:2, one launch (start us, length us, event | category | flops | bytes accessed | tf_op | source)
XLA Modules:
  0.0 65.1 jit_solution(7804269381242162887)
XLA Ops:
  0.0 0.0 copy-start
  0.0 1.4 %copy.11 = f32[4,8,4,12,128]{4,1,3,2,0:T(8,128)S(1)} copy(f32[4,8,4,12,128]{4,2,3,1,0:T(4,128)} %bitcast.12) | data formatting | bytes 1572864 | tf_op jit(solution)/shard_map/reshape | solution.py:316
  1.4 0.0 copy-done
  1.4 62.3 %shard_map.28 = f32[48,32,128]{2,1,0:T(8,128)S(1)} custom-call(f32[4,4,12,8,128]{4,3,2,1,0:T(8,128)S(1)} %bitcast.10, f32[12,4,128]{2,1,0:T(4,128)S(1)} %bitcast.11), custom_call_target="tpu_custom_call" | custom-call | tf_op jit(solution)/shard_map/pallas_call | solution.py:318
  63.8 1.4 %copy.12 = f32[4,12,32,128]{3,0,1,2:T(4,128)} copy(f32[4,12,32,128]{3,2,1,0:T(8,128)S(1)} %bitcast.9) | data formatting | bytes 1572864 | tf_op jit(solution)/shard_map/reshape | solution.py:339
Async XLA Ops:
  0.0 1.4 %copy-start = (f32[4,12,128]{2,0,1:T(4,128)S(1)}, f32[4,12,128]{2,0,1:T(4,128)}, u32[]{:S(2)}) copy-start(f32[4,12,128]{2,0,1:T(4,128)} %param.3) | copy-start | bytes 73732

commit v3 on v2

--- a/solution.py
+++ b/solution.py
@@ -176,10 +176,10 @@
     def halo2(c, side):
         return halo(ext2.at[c, own], ext2, send2, recv2, c, side)
 
-    def across(c):
+    def across(c, p):
         return pltpu.make_async_remote_copy(
-            src_ref=fil.at[c], dst_ref=fil0.at[c],
-            send_sem=sendx.at[c], recv_sem=recvx.at[c],
+            src_ref=fil.at[c, pl.ds(p * ny, ny)], dst_ref=fil0.at[c, pl.ds(p * ny, ny)],
+            send_sem=sendx.at[c, p], recv_sem=recvx.at[c, p],
             device_id=partner, device_id_type=MESH,
         )
 
@@ -208,40 +208,58 @@
         for p in range(planes):
             value = 2.0 * chebyshev_step(ext2, pot_ref, c, p) - ext[c, 4 + p]
             fil[c, pl.ds(p * ny, ny)] = value
+            send_across(c, p)
 
         @pl.when(band == 0)
         def _():
-            across(c).start()
             fil0[c] = fil[c]
 
         return carry
 
+    def send_across(c, p):
+        @pl.when(band == 0)
+        def _():
+            across(c, p).start()
+
     lax.fori_loop(0, chunks, second, 0)
-
-    @pl.when(band == 1)
-    def _():
-        for c in range(chunks):
-            across(c).wait_recv()
 
     rows = chunks * ROWS
     size = 2 * rows
 
-    def pair(i):
-        def at(ref, line):
-            return ref[:, line].reshape(rows, ref.shape[3])
-
-        return jnp.concatenate(
-            [
-                jnp.concatenate([at(fil0, 2 * i + t), at(fil, 2 * i + t)], axis=0)
-                for t in range(2)
-            ],
-            axis=1,
-        )
+    def cast(ref, low_chunk, high_chunk, start):
+        count = (high_chunk - low_chunk) * ROWS
+
+        def one(i, carry):
+            value = jnp.concatenate(
+                [
+                    ref[low_chunk:high_chunk, 2 * i + t].reshape(count, ref.shape[3])
+                    for t in range(2)
+                ],
+                axis=1,
+            )
+            high, low = split(value)
+            both[i, start : start + count] = high
+            both[i, size + start : size + start + count] = low
+            return carry
+
+        lax.fori_loop(0, lines // 2, one, 0, unroll=4)
+
+    def arrived(low_chunk, high_chunk):
+        @pl.when(band == 1)
+        def _():
+            for c in range(low_chunk, high_chunk):
+                for p in range(planes):
+                    across(c, p).wait_recv()
+
+    half_way = chunks // 2
+    cast(fil, 0, chunks, rows)
+    arrived(0, half_way)
+    cast(fil0, 0, half_way, 0)
+    arrived(half_way, chunks)
+    cast(fil0, half_way, chunks, half_way * ROWS)
 
     def gram(i, total):
-        high, low = split(pair(i))
-        tall = jnp.concatenate([high, low], axis=0)
-        both[i] = tall
+        tall = both[i]
         return total + lax.dot_general(
             tall, tall, (((1,), (1,)), ((), ())), preferred_element_type=jnp.float32
         )
@@ -252,6 +270,8 @@
     total = total[:size] + total[size:]
     total = total[:, :size] + total[:, size:]
     packed = jnp.concatenate([total[:rows], total[rows:]], axis=1)
+
+    sent = []
 
     def exchange(value, slots, send, recv, place, peers, sources):
         slots[place] = value
@@ -265,14 +285,13 @@
         ]
         for copy in copies:
             copy.start()
-        for copy in copies:
-            copy.wait_send()
         for k, source in enumerate(sources):
             pltpu.make_async_remote_copy(
                 src_ref=slots.at[source], dst_ref=slots.at[source],
                 send_sem=send.at[k], recv_sem=recv.at[k],
                 device_id={"grid": peers[k]}, device_id_type=MESH,
             ).wait_recv()
+        sent.extend(copies)
         out = slots[0]
         for k in range(1, slots.shape[0]):
             out = out + slots[k]
@@ -299,6 +318,8 @@
 
     lax.fori_loop(0, lines // 2, final, 0, unroll=UNROLL)
 
+    for copy in sent:
+        copy.wait_send()
     for c in range(chunks):
         for side in range(2):
             halo1(c, side).wait_send()
@@ -307,7 +328,8 @@
     @pl.when(band == 0)
     def _():
         for c in range(chunks):
-            across(c).wait_send()
+            for p in range(planes):
+                across(c, p).wait_send()
 
 
 def on_device_two(n, orbitals, potential):
@@ -329,7 +351,7 @@
             pltpu.VMEM((4, rows, 4 * rows), f32),
             pltpu.VMEM((n // 4, rows, 4 * rows), f32),
             dma((2, chunks)), dma((2, chunks)), dma((2, chunks)), dma((2, chunks)),
-            dma((chunks,)), dma((chunks,)),
+            dma((chunks, planes)), dma((chunks, planes)),
             dma((3,)), dma((3,)), dma((n // 4 - 1,)), dma((n // 4 - 1,)),
         ],
         compiler_params=pltpu.CompilerParams(

time: 65.3 us -> 65.2 us (level)
  no operation moved by 1% of the time
where the time goes in v3:
time: 65.2 us; the launch traced here: 65.1 us
  Pallas kernels  62.3 us (96%)
  local copies, waits for them, and re-layouts  2.77 us (4%)
    pallas_call x1, Pallas kernels, on_device_two(): pl.pallas_call(functools.partial(kernel, n), out_shape=jax.ShapeDtypeStru...  62.3 us
    reshape x1, local copies, waits for them, and re-layouts, on_device_two(): return out.reshape(planes, ny, rows, nz).transpose(2, 0, 1, 3)  1.39 us
    reshape x1, local copies, waits for them, and re-layouts, on_device_two(): x = orbitals.reshape(chunks, ROWS, planes, ny, nz).transpose(0, 2, 3, 1, 4)  1.38 us

profile of v3, /device:TPU:2, one launch (start us, length us, event | category | flops | bytes accessed | tf_op | source)
XLA Modules:
  0.0 65.1 jit_solution(5213438764440292949)
XLA Ops:
  0.0 0.0 copy-start
  0.0 1.4 %copy.11 = f32[4,8,4,12,128]{4,1,3,2,0:T(8,128)S(1)} copy(f32[4,8,4,12,128]{4,2,3,1,0:T(4,128)} %bitcast.12) | data formatting | bytes 1572864 | tf_op jit(solution)/shard_map/reshape | solution.py:338
  1.4 0.0 copy-done
  1.4 62.3 %shard_map.28 = f32[48,32,128]{2,1,0:T(8,128)S(1)} custom-call(f32[4,4,12,8,128]{4,3,2,1,0:T(8,128)S(1)} %bitcast.10, f32[12,4,128]{2,1,0:T(4,128)S(1)} %bitcast.11), custom_call_target="tpu_custom_call" | custom-call | tf_op jit(solution)/shard_map/pallas_call | solution.py:340
  63.7 1.4 %copy.12 = f32[4,12,32,128]{3,0,1,2:T(4,128)} copy(f32[4,12,32,128]{3,2,1,0:T(8,128)S(1)} %bitcast.9) | data formatting | bytes 1572864 | tf_op jit(solution)/shard_map/reshape | solution.py:361
Async XLA Ops:
  0.0 1.4 %copy-start = (f32[4,12,128]{2,0,1:T(4,128)S(1)}, f32[4,12,128]{2,0,1:T(4,128)}, u32[]{:S(2)}) copy-start(f32[4,12,128]{2,0,1:T(4,128)} %param.3) | copy-start | bytes 73732

commit v4 on v3

--- a/solution.py
+++ b/solution.py
@@ -107,24 +107,13 @@
     unit = jnp.where(unit_rows == unit_lanes, 1.0, 0.0).astype(jnp.float32)
     whole = jnp.concatenate([gram, unit], axis=1)
     blocks = [whole[ROWS * k : ROWS * (k + 1)] for k in range(size // ROWS)]
-    for j in range(0, size, 2):
+    for j in range(size):
         own, at = divmod(j, ROWS)
-        row0, row1 = blocks[own][at : at + 1], blocks[own][at + 1 : at + 2]
-        scale = 1.0 / row0[:, j : j + 1]
-        across = row0[:, j + 1 : j + 2]
-        ratio = row1[:, j : j + 1] * scale
-        row1_left = row1 - ratio * row0
-        cross = across * scale
-        unit0 = row0 * scale
-        unit1 = row1_left / (row1[:, j + 1 : j + 2] - ratio * across)
+        row = blocks[own][at : at + 1]
+        row = row / row[:, j : j + 1]
         for k in range(own, size // ROWS):
-            col0 = blocks[k][:, j : j + 1]
-            col1 = blocks[k][:, j + 1 : j + 2] - col0 * cross
-            less = blocks[k] - col0 * unit0 - col1 * unit1
-            if k == own:
-                less = jnp.where(rows > at + 1, less, blocks[k])
-                less = jnp.where(rows == at + 1, row1_left, less)
-            blocks[k] = less
+            less = blocks[k] - blocks[k][:, j : j + 1] * row
+            blocks[k] = jnp.where(rows > at, less, blocks[k]) if k == own else less
     scaled = []
     for k, block in enumerate(blocks):
         pivot = jnp.sum(jnp.where(lanes == rows + ROWS * k, block, 0.0), axis=1, keepdims=True)

time: 65.2 us -> 61.6 us (0.945)
  Pallas kernels: 62.3 us -> 58.7 us
    pallas_call x1, Pallas kernels: 62.3 us -> 58.7 us  [on_device_two(): pl.pallas_call(functools.partial(kernel, n), out_shape=jax.ShapeDtypeStru...]
where the time goes in v4:
time: 61.6 us; the launch traced here: 61.4 us
  Pallas kernels  58.7 us (95%)
  local copies, waits for them, and re-layouts  2.77 us (4%)
    pallas_call x1, Pallas kernels, on_device_two(): pl.pallas_call(functools.partial(kernel, n), out_shape=jax.ShapeDtypeStru...  58.7 us
    reshape x1, local copies, waits for them, and re-layouts, on_device_two(): return out.reshape(planes, ny, rows, nz).transpose(2, 0, 1, 3)  1.39 us
    reshape x1, local copies, waits for them, and re-layouts, on_device_two(): x = orbitals.reshape(chunks, ROWS, planes, ny, nz).transpose(0, 2, 3, 1, 4)  1.38 us

profile of v4, /device:TPU:2, one launch (start us, length us, event | category | flops | bytes accessed | tf_op | source)
XLA Modules:
  0.0 61.4 jit_solution(12453218751450132354)
XLA Ops:
  0.0 0.0 copy-start
  0.0 1.4 %copy.11 = f32[4,8,4,12,128]{4,1,3,2,0:T(8,128)S(1)} copy(f32[4,8,4,12,128]{4,2,3,1,0:T(4,128)} %bitcast.12) | data formatting | bytes 1572864 | tf_op jit(solution)/shard_map/reshape | solution.py:327
  1.4 0.0 copy-done
  1.4 58.7 %shard_map.28 = f32[48,32,128]{2,1,0:T(8,128)S(1)} custom-call(f32[4,4,12,8,128]{4,3,2,1,0:T(8,128)S(1)} %bitcast.10, f32[12,4,128]{2,1,0:T(4,128)S(1)} %bitcast.11), custom_call_target="tpu_custom_call" | custom-call | tf_op jit(solution)/shard_map/pallas_call | solution.py:329
  60.1 1.4 %copy.12 = f32[4,12,32,128]{3,0,1,2:T(4,128)} copy(f32[4,12,32,128]{3,2,1,0:T(8,128)S(1)} %bitcast.9) | data formatting | bytes 1572864 | tf_op jit(solution)/shard_map/reshape | solution.py:350
Async XLA Ops:
  0.0 1.4 %copy-start = (f32[4,12,128]{2,0,1:T(4,128)S(1)}, f32[4,12,128]{2,0,1:T(4,128)}, u32[]{:S(2)}) copy-start(f32[4,12,128]{2,0,1:T(4,128)} %param.3) | copy-start | bytes 73732

commit v5 on v4

--- a/solution.py
+++ b/solution.py
@@ -11,7 +11,7 @@
 MIDDLE = 6.875
 SPREAD = 3.875
 ROWS = 8
-UNROLL = 12
+UNROLL = 24
 MESH = pl.DeviceIdType.MESH
 
 
@@ -231,7 +231,7 @@
             both[i, size + start : size + start + count] = low
             return carry
 
-        lax.fori_loop(0, lines // 2, one, 0, unroll=4)
+        lax.fori_loop(0, lines // 2, one, 0, unroll=12)
 
     def arrived(low_chunk, high_chunk):
         @pl.when(band == 1)

time: 61.6 us -> 61.6 us (level)
  no operation moved by 1% of the time
where the time goes in v5:
time: 61.6 us; the launch traced here: 61.4 us
  Pallas kernels  58.6 us (95%)
  local copies, waits for them, and re-layouts  2.77 us (4%)
    pallas_call x1, Pallas kernels, on_device_two(): pl.pallas_call(functools.partial(kernel, n), out_shape=jax.ShapeDtypeStru...  58.6 us
    reshape x1, local copies, waits for them, and re-layouts, on_device_two(): return out.reshape(planes, ny, rows, nz).transpose(2, 0, 1, 3)  1.39 us
    reshape x1, local copies, waits for them, and re-layouts, on_device_two(): x = orbitals.reshape(chunks, ROWS, planes, ny, nz).transpose(0, 2, 3, 1, 4)  1.38 us

profile of v5, /device:TPU:2, one launch (start us, length us, event | category | flops | bytes accessed | tf_op | source)
XLA Modules:
  0.0 61.4 jit_solution(470358554937681702)
XLA Ops:
  0.0 0.0 copy-start
  0.0 1.4 %copy.11 = f32[4,8,4,12,128]{4,1,3,2,0:T(8,128)S(1)} copy(f32[4,8,4,12,128]{4,2,3,1,0:T(4,128)} %bitcast.12) | data formatting | bytes 1572864 | tf_op jit(solution)/shard_map/reshape | solution.py:327
  1.4 0.0 copy-done
  1.4 58.6 %shard_map.28 = f32[48,32,128]{2,1,0:T(8,128)S(1)} custom-call(f32[4,4,12,8,128]{4,3,2,1,0:T(8,128)S(1)} %bitcast.10, f32[12,4,128]{2,1,0:T(4,128)S(1)} %bitcast.11), custom_call_target="tpu_custom_call" | custom-call | tf_op jit(solution)/shard_map/pallas_call | solution.py:329
  60.1 1.4 %copy.12 = f32[4,12,32,128]{3,0,1,2:T(4,128)} copy(f32[4,12,32,128]{3,2,1,0:T(8,128)S(1)} %bitcast.9) | data formatting | bytes 1572864 | tf_op jit(solution)/shard_map/reshape | solution.py:350
Async XLA Ops:
  0.0 1.4 %copy-start = (f32[4,12,128]{2,0,1:T(4,128)S(1)}, f32[4,12,128]{2,0,1:T(4,128)}, u32[]{:S(2)}) copy-start(f32[4,12,128]{2,0,1:T(4,128)} %param.3) | copy-start | bytes 73732
